TPU v7x, 32 devices: a whole 2x2x4 slice. The times are simulated.
32 devices in a mesh: row: 4 (over y, x), col: 8 (over z, core).
Axes of the slice: x: 2, y: 2, z: 4, core: 2. Of those that a mesh axis runs over, the one named last changes fastest.
Arguments:
- inverse_sep: float32 [12288, 12288], P('row', 'col'), may hold values from -105 to 105, as said below
- sep_panels: float32 [3, 12288, 256], P(None, 'row', 'col'), may hold values from -0.0546875 to 0.0546875
- chain_panels: float32 [3, 256, 256], P(None, 'row', 'col'), may hold values from -0.375 to 0.375
- diag_inverse: float32 [3, 256, 256], P(None, 'row'), may hold values from -5 to 5, as said below
- tile_list: int32 [3, 96], replicated, may hold values from 0 to 1, as said below
Outputs:
- sep_rows: float32 [3, 256, 12288], P(None, 'row', 'col')
- chain_inverse: float32 [3, 256, 768], P(None, 'row')
Inputs may be any that keep to these rules, and one draw needn't show every extreme that they name: `inverse_sep`: symmetric. `diag_inverse`: each block symmetric. `tile_list`: a tile listed for supernode k is listed for every earlier supernode.
All inputs are finite; a program needn't handle non-finite values.
Results may differ from a plain program's by a relative error of at most 0.00013.
Values sent between devices are 32-bit elements; how exact they have to be, the bound alone decides.
A program may use at most 128 MiB of HBM per device.

v0:
```python
import jax
import jax.numpy as jnp
from jax import lax
from jax.sharding import PartitionSpec as P

NB = 256
TILE = 128
NSUPER = 3


def broadcast(block, axis, source):
    block = jnp.where(lax.axis_index(axis) == source, block, jnp.zeros_like(block))
    return lax.psum(block, axis)


def pair_index(current, earlier):
    return current * (current - 1) // 2 + earlier


def product(left, right):
    return jnp.dot(left, right, precision=lax.Precision.HIGHEST, preferred_element_type=jnp.float32)


def inner_product(left, right):
    return lax.dot_general(
        left,
        right,
        (((0,), (0,)), ((), ())),
        precision=lax.Precision.HIGHEST,
        preferred_element_type=jnp.float32,
    )


def per_device(inverse_sep, sep_panels, chain_panels, diag_inverse, tile_list):
    row_count = lax.axis_size("row")
    col_count = lax.axis_size("col")
    row_place = lax.axis_index("row")
    col_place = lax.axis_index("col")
    row_cells, col_cells = inverse_sep.shape
    nb_rows = NB // row_count
    nb_cols = NB // col_count
    ratio_cols = col_count // row_count
    root_row = col_place // ratio_cols
    inner_part = col_place % ratio_cols
    tile_rows = row_cells // TILE
    listed = lax.dynamic_slice_in_dim(tile_list, row_place * tile_rows, tile_rows, 1).astype(
        jnp.float32
    )

    def own_cols(panel):
        return lax.dynamic_slice_in_dim(panel, inner_part * col_cells, col_cells, 0)

    def own_chain(rows_block):
        return lax.dynamic_slice_in_dim(rows_block, inner_part * nb_cols, nb_cols, 0)

    panels = [None] * NSUPER
    column_panels = [None] * NSUPER
    chain_rowlay = [None] * NSUPER
    chain_colrows = [None] * NSUPER
    gathered, chains = (
        lax.all_gather(sep_panels, "col", axis=2, tiled=True),
        lax.all_gather(chain_panels, "col", axis=2, tiled=True),
    )
    for current in range(NSUPER):
        masked_panel = gathered[current]
        panels[current] = (
            masked_panel.reshape(tile_rows, TILE, NB) * listed[current][:, None, None]
        ).reshape(row_cells, NB)
        chain_rowlay[current] = chains[current]
    local_cols = jnp.stack([own_cols(panel) for panel in panels])
    payload = jnp.concatenate(
        [local_cols, jnp.stack([own_chain(block) for block in chain_rowlay])], axis=1
    )
    shared = broadcast(payload, "row", root_row)
    for current in range(NSUPER):
        column_panels[current] = shared[current, :col_cells]
        chain_colrows[current] = shared[current, col_cells:]
    state = jnp.zeros((NSUPER, nb_rows, NSUPER * NB), jnp.float32)
    new_rows = []
    for current in range(NSUPER):
        panel = panels[current]
        earlier_pairs = [
            (chain_rowlay[pair_index(current, earlier)], new_rows[earlier])
            for earlier in range(current)
        ]
        summed = inner_product(panel, inverse_sep)
        for chain_block, old_rows in earlier_pairs:
            summed = summed + inner_product(chain_block, old_rows)
        rows_now = -lax.psum_scatter(summed, "row", scatter_dimension=0, tiled=True)
        col_panel = column_panels[current]
        parts = [product(rows_now, col_panel)]
        for earlier in range(current):
            crossed = product(new_rows[earlier], col_panel)
            for middle in range(current):
                state_cols = lax.dynamic_slice_in_dim(
                    state[earlier], middle * NB + col_place * nb_cols, nb_cols, 1
                )
                crossed = crossed + product(state_cols, chain_colrows[pair_index(current, middle)])
            parts.append(crossed)
        totals = lax.psum(jnp.stack(parts), "col")
        first_term = totals[0]
        crossing = [-totals[1 + earlier] for earlier in range(current)]
        second_term = jnp.zeros((nb_rows, NB), jnp.float32)
        if current > 0:
            mirrored = jnp.swapaxes(
                lax.all_to_all(jnp.stack(crossing), "row", split_axis=2, concat_axis=1, tiled=True),
                1,
                2,
            )
            partial_sum = jnp.zeros((nb_rows, NB), jnp.float32)
            for earlier in range(current):
                mirror_cols = lax.dynamic_slice_in_dim(
                    mirrored[earlier], col_place * nb_cols, nb_cols, 1
                )
                partial_sum = partial_sum + product(
                    mirror_cols, chain_colrows[pair_index(current, earlier)]
                )
            second_term = lax.psum(partial_sum, "col")
            for earlier in range(current):
                state = state.at[earlier, :, current * NB : (current + 1) * NB].set(
                    crossing[earlier]
                )
                state = state.at[current, :, earlier * NB : (earlier + 1) * NB].set(
                    mirrored[earlier]
                )
        state = state.at[current, :, current * NB : (current + 1) * NB].set(
            diag_inverse[current] - first_term - second_term
        )
        new_rows.append(rows_now)
    return (jnp.stack(new_rows), state)


def solution(mesh):
    in_specs = (
        P("row", "col"),
        P(None, "row", "col"),
        P(None, "row", "col"),
        P(None, "row", None),
        P(),
    )
    out_specs = (P(None, "row", "col"), P(None, "row", None))
    return jax.shard_map(
        per_device, mesh=mesh, in_specs=in_specs, out_specs=out_specs, check_vma=False
    )
```

profile of v0, /device:TPU:0, one launch (start us, length us, event | category | flops | bytes accessed | tf_op | source)
XLA Modules:
  0.0 669.9 jit_solution(11493135787180381727)
XLA Ops:
  8.9 94.2 %all-gather.2.cloned.1.call-done = f32[3,3072,256]{1,2,0:T(8,128)} async-done(((f32[3,3072,32]{1,2,0:T(8,128)}), f32[3,3072,256]{1,2,0:T(8,128)}) %all-gather.2.cloned.1.call-update) | async-done | bytes 9437200 | tf_op jit(solution)/shard_map/all_gather | solution.py:61
  103.1 6.6 fusion.1
  111.3 20.0 %fusion.86 = f32[256,1536]{1,0:T(8,128)} fusion(f32[3072,256]{0,1:T(8,128)S(1)} %get-tuple-element.114, f32[3072,1536]{1,0:T(8,128)} %param.23), kind=kOutput, calls=%fused_computation.141 | convolution fusion | flops 14495514624 | bytes 23592960 | tf_op jit(solution)/shard_map/dot_general | solution.py:25
  131.4 14.5 %all_gather.7 = f32[3,64,256]{1,2,0:T(8,128)S(1)} all-gather(f32[3,64,32]{1,2,0:T(8,128)S(1)} %copy-done.9), channel_id=1, replica_groups=mesh['row'=4,'col'=8] {'col'}, dimensions={2}, use_global_device_ids=true | all-gather | bytes 221184 | tf_op jit(solution)/shard_map/all_gather | solution.py:62
  152.1 20.9 %fusion.87 = f32[256,1536]{1,0:T(8,128)} fusion(f32[3072,256]{0,1:T(8,128)} %get-tuple-element.112, f32[3072,1536]{1,0:T(8,128)} %param.23), kind=kOutput, calls=%fused_computation.142 | convolution fusion | flops 14495514624 | bytes 23592960 | tf_op jit(solution)/shard_map/dot_general | solution.py:25
  173.1 110.2 %all-reduce.8.cloned.1.call-done = f32[3,1568,256]{1,2,0:T(8,128)} async-done(((f32[3,1568,256]{1,2,0:T(8,128)}), f32[3,1568,256]{1,2,0:T(8,128)}) %all-reduce.8.cloned.1.call-update) | async-done | bytes 4816912 | tf_op jit(solution)/shard_map/psum | solution.py:13
  283.3 3.7 fusion.22
  287.1 4.2 fusion.5
  292.3 3.2 and_reduce_fusion
  295.5 45.3 %all-reduce.10.cloned.1.call-done = f32[1,64,256]{2,1,0:T(8,128)} async-done(((f32[1,64,256]{2,1,0:T(8,128)}), f32[1,64,256]{2,1,0:T(8,128)}) %all-reduce.10.cloned.1.call-update) | async-done | bytes 65552 | tf_op jit(solution)/shard_map/psum | solution.py:100
  343.5 3.6 fusion.21
  347.1 26.7 %reduce-scatter.6.cloned.1.call-done = f32[64,1536]{1,0:T(8,128)} async-done(((f32[256,1536]{1,0:T(8,128)}), f32[64,1536]{1,0:T(8,128)}) %reduce-scatter.6.cloned.1.call-update) | async-done | bytes 393232 | tf_op jit(solution)/shard_map/reduce_scatter | solution.py:89
  373.8 3.1 fusion.19
  378.5 20.0 %fusion.88 = f32[256,1536]{1,0:T(8,128)} fusion(f32[3072,256]{0,1:T(8,128)S(1)} %get-tuple-element.113, f32[3072,1536]{1,0:T(8,128)} %param.23), kind=kOutput, calls=%fused_computation.143 | convolution fusion | flops 14495514624 | bytes 23592960 | tf_op jit(solution)/shard_map/dot_general | solution.py:25
  398.5 34.4 %all-reduce.12.cloned.1.call-done = f32[2,64,256]{2,1,0:T(8,128)} async-done(((f32[2,64,256]{2,1,0:T(8,128)}), f32[2,64,256]{2,1,0:T(8,128)}) %all-reduce.12.cloned.1.call-update) | async-done | bytes 131088 | tf_op jit(solution)/shard_map/psum | solution.py:100
  438.0 3.6 all-to-all-start
  449.9 3.5 fusion.3
  455.6 45.4 %all-reduce.14.cloned.1.call-done = f32[64,256]{1,0:T(8,128)} async-done(((f32[64,256]{1,0:T(8,128)}), f32[64,256]{1,0:T(8,128)}) %all-reduce.14.cloned.1.call-update) | async-done | bytes 65552 | tf_op jit(solution)/shard_map/psum | solution.py:118
  509.7 3.0 fusion.15
  512.7 21.5 %reduce-scatter.8.cloned.1.call-done = f32[64,1536]{1,0:T(8,128)} async-done(((f32[256,1536]{1,0:T(8,128)}), f32[64,1536]{1,0:T(8,128)}) %reduce-scatter.8.cloned.1.call-update) | async-done | bytes 393232 | tf_op jit(solution)/shard_map/reduce_scatter | solution.py:89
  534.2 3.1 fusion.12
  539.1 53.7 %all-reduce.16.cloned.1.call-done = f32[3,64,256]{2,1,0:T(8,128)} async-done(((f32[3,64,256]{2,1,0:T(8,128)}), f32[3,64,256]{2,1,0:T(8,128)}) %all-reduce.16.cloned.1.call-update) | async-done | bytes 196624 | tf_op jit(solution)/shard_map/psum | solution.py:100
  596.7 3.6 all-to-all-start.1
  610.1 51.3 %all-reduce.18.cloned.1.call-done = f32[64,256]{1,0:T(8,128)} async-done(((f32[64,256]{1,0:T(8,128)}), f32[64,256]{1,0:T(8,128)}) %all-reduce.18.cloned.1.call-update) | async-done | bytes 65552 | tf_op jit(solution)/shard_map/psum | solution.py:118
  (104 shorter events, 55.9 us)
Async XLA Ops:
  7.2 95.9 %all-gather.2.cloned.1.call-start = ((), (), s32[]{:S(2)}) async-start(), calls=%async_computation.5 | async-start | bytes 10616832 | tf_op jit(solution)/shard_map/all_gather | solution.py:61
  7.9 165.2 %reduce-scatter.4.cloned.1.call-start = ((), (), s32[]{:S(2)}) async-start(), calls=%async_computation.6 | async-start | bytes 1966080 | tf_op jit(solution)/shard_map/reduce_scatter | solution.py:89
  109.7 1.6 copy-start.1
  111.3 20.1 %copy-start.9 = (f32[3,64,32]{1,2,0:T(8,128)S(1)}, f32[3,64,32]{1,2,0:T(8,128)}, u32[]{:S(2)}) copy-start(f32[3,64,32]{1,2,0:T(8,128)} %param.25) | copy-start | bytes 73732
  131.3 151.9 %all-reduce.8.cloned.1.call-start = ((), (), s32[]{:S(2)}) async-start(), calls=%async_computation.9 | async-start | bytes 10223616 | tf_op jit(solution)/shard_map/psum | solution.py:13
  145.9 0.7 copy-start.4
  146.8 2.4 copy-start
  151.9 188.9 %all-reduce.10.cloned.1.call-start = ((), (), s32[]{:S(2)}) async-start(), calls=%async_computation.10 | async-start | bytes 131072 | tf_op jit(solution)/shard_map/psum | solution.py:100
  287.0 5.3 copy-start.10
  287.0 56.5 %copy-start.2 = (f32[64,1536]{1,0:T(8,128)S(1)}, f32[64,1536]{1,0:T(8,128)}, u32[]{:S(2)}) copy-start(f32[64,1536]{1,0:T(8,128)} %reduce-scatter.4.cloned.1.call-done) | copy-start | bytes 1179652
  287.0 86.8 %reduce-scatter.6.cloned.1.call-start = ((), (), s32[]{:S(2)}) async-start(), calls=%async_computation.7 | async-start | bytes 1966080 | tf_op jit(solution)/shard_map/reduce_scatter | solution.py:89
  291.3 141.5 %all-reduce.12.cloned.1.call-start = ((), (), s32[]{:S(2)}) async-start(), calls=%async_computation.11 | async-start | bytes 262144 | tf_op jit(solution)/shard_map/psum | solution.py:100
  341.7 0.6 copy-start.6
  398.4 51.5 %copy-start.3 = (f32[64,1536]{1,0:T(8,128)S(1)}, f32[64,1536]{1,0:T(8,128)}, u32[]{:S(2)}) copy-start(f32[64,1536]{1,0:T(8,128)} %reduce-scatter.6.cloned.1.call-done) | copy-start | bytes 1179652
  438.0 8.5 %all-to-all-start = ((f32[4,1,4096]{2,1,0:T(1,128)}), f32[4,1,4096]{2,1,0:T(1,128)S(1)}, u32[]{:S(2)}, u32[]{:S(2)}) async-start(f32[4,1,4096]{2,1,0:T(1,128)} %reshape.358), calls=%async_computation.3 | async-start | bytes 131072 | tf_op jit(solution)/shard_map/all_to_all | solution.py:106
  441.7 59.3 %all-reduce.14.cloned.1.call-start = ((), (), s32[]{:S(2)}) async-start(), calls=%async_computation.12 | async-start | bytes 131072 | tf_op jit(solution)/shard_map/psum | solution.py:118
  447.7 5.8 copy-start.7
  449.6 84.6 %reduce-scatter.8.cloned.1.call-start = ((), (), s32[]{:S(2)}) async-start(), calls=%async_computation.8 | async-start | bytes 1966080 | tf_op jit(solution)/shard_map/reduce_scatter | solution.py:89
  453.5 139.3 %all-reduce.16.cloned.1.call-start = ((), (), s32[]{:S(2)}) async-start(), calls=%async_computation.13 | async-start | bytes 393216 | tf_op jit(solution)/shard_map/psum | solution.py:100
  595.6 14.4 %copy-start.8 = (f32[3,64,256]{2,1,0:T(8,128)S(1)}, f32[3,64,256]{2,1,0:T(8,128)}, u32[]{:S(2)}) copy-start(f32[3,64,256]{2,1,0:T(8,128)} %all-reduce.16.cloned.1.call-done) | copy-start | bytes 589828
  596.7 8.7 %all-to-all-start.1 = ((f32[4,1,8192]{2,1,0:T(1,128)}), f32[4,1,8192]{2,1,0:T(1,128)S(1)}, u32[]{:S(2)}, u32[]{:S(2)}) async-start(f32[4,1,8192]{2,1,0:T(1,128)} %reshape.360), calls=%async_computation.4 | async-start | bytes 262144 | tf_op jit(solution)/shard_map/all_to_all | solution.py:106
  600.3 61.0 %all-reduce.18.cloned.1.call-start = ((), (), s32[]{:S(2)}) async-start(), calls=%async_computation.14 | async-start | bytes 131072 | tf_op jit(solution)/shard_map/psum | solution.py:118
  662.2 0.8 copy-start.5
Sparse Core Ops, SparseCore 0:
  9.6 93.4 all-gather.1
  131.5 29.3 reduce-scatter.3
  164.3 118.9 all-reduce.7
  287.1 53.5 all-reduce.9
  343.9 29.8 reduce-scatter.5
  378.6 54.2 all-reduce.11
  449.7 51.1 all-reduce.13
  504.2 29.9 reduce-scatter.7
  538.2 54.5 all-reduce.15
  610.2 51.1 all-reduce.17
where the time goes:
time: 671 us; the launch traced here: 670 us
  waiting for transfers between devices  488 us (73%)
  matrix products  102 us (15%)
  other arithmetic  28.5 us (4%)
  blocking collectives  14.5 us (2%)
  between operations  14.5 us (2%)
  local copies, waits for them, and re-layouts  14.4 us (2%)
  starting transfers between devices  8.29 us (1%)
    psum x3, waiting for transfers between devices, per_device(): totals = lax.psum(jnp.stack(parts), 'col')  133 us
    psum x1, waiting for transfers between devices, broadcast(): return lax.psum(block, axis)  110 us
    psum x2, waiting for transfers between devices, per_device(): second_term = lax.psum(partial_sum, 'col')  96.6 us
    all_gather x1, waiting for transfers between devices, per_device(): lax.all_gather(sep_panels, 'col', axis=2, tiled=True)  94.2 us
    dot_general x6, matrix products, inner_product(): lax.dot_general(left, right, (((0,), (0,)), ((), ())), precision=lax.Prec...  71.5 us
    reduce_scatter x3, waiting for transfers between devices, per_device(): rows_now = -lax.psum_scatter(summed, 'row', scatter_dimension=0, tiled=True)  48.2 us
    dot_general x14, matrix products, product(): jnp.dot(left, right, precision=lax.Precision.HIGHEST, preferred_element_t...  30.4 us
    all_gather x1, blocking collectives, per_device(): lax.all_gather(chain_panels, 'col', axis=2, tiled=True)  14.5 us
  transfers between devices with their start and end apart: 12, of which 11 were waited for; matrix products, arithmetic and copies ran while one was open for 13% of the time, Pallas kernels for 0%

commit v1 on v0

v1 whole, which is shorter than its diff:
```python
import jax
import jax.numpy as jnp
from jax import lax
from jax.sharding import PartitionSpec as P

NB = 256
TILE = 128
NSUPER = 3


def pair_index(current, earlier):
    return current * (current - 1) // 2 + earlier


def dot(left, right, left_dim, right_dim, precision=lax.Precision.HIGH):
    return lax.dot_general(
        left,
        right,
        (((left_dim,), (right_dim,)), ((), ())),
        precision=precision,
        preferred_element_type=jnp.float32,
    )


def finish(total, chain, diag):
    highest = lax.Precision.HIGHEST
    blocks = {}
    for current in range(NSUPER):
        crossing = []
        for earlier in range(current):
            crossed = total[earlier, current]
            for middle in range(current):
                crossed = crossed + dot(
                    blocks[earlier, middle], chain[pair_index(current, middle)], 1, 0, highest
                )
            crossing.append(-crossed)
        own = diag[current] - total[current, current]
        for earlier in range(current):
            blocks[earlier, current] = crossing[earlier]
            blocks[current, earlier] = crossing[earlier].T
            own = own - dot(
                crossing[earlier], chain[pair_index(current, earlier)], 0, 0, highest
            )
        blocks[current, current] = own
    return jnp.stack(
        [
            jnp.concatenate([blocks[line, column] for column in range(NSUPER)], axis=1)
            for line in range(NSUPER)
        ]
    )


def per_device(inverse_sep, sep_panels, chain_panels, diag_inverse, tile_list):
    row_count = lax.axis_size("row")
    col_count = lax.axis_size("col")
    row_place = lax.axis_index("row")
    col_place = lax.axis_index("col")
    row_cells, col_cells = inverse_sep.shape
    nb_rows = NB // row_count
    nb_cols = NB // col_count
    ratio_cols = col_count // row_count
    root_row = col_place // ratio_cols
    inner_part = col_place % ratio_cols
    tile_rows = row_cells // TILE
    listed = lax.dynamic_slice_in_dim(tile_list, row_place * tile_rows, tile_rows, 1)
    listed = jnp.repeat(listed.astype(jnp.float32), TILE, axis=1)

    local = jnp.swapaxes(sep_panels, 1, 2) * listed[:, None, :]
    panels = [
        lax.all_gather(local[current], "col", axis=0, tiled=True) for current in range(NSUPER)
    ]
    diag_part = lax.dynamic_slice_in_dim(diag_inverse, col_place * nb_cols, nb_cols, 2)
    small = jnp.stack([chain_panels, diag_part]).reshape(-1, 128)
    small = lax.all_gather(small, ("row", "col"), axis=0, tiled=False)
    small = small.reshape(row_count, col_count, 2, NSUPER, nb_rows, nb_cols)
    small = small.transpose(2, 3, 0, 4, 1, 5).reshape(2, NSUPER, NB, NB)
    chain, diag = small[0], small[1]

    is_root = row_place == root_row
    partial = []
    rows = []
    total = {}
    for current in range(NSUPER):
        summed = -dot(panels[current], inverse_sep, 1, 0)
        for earlier in range(current):
            summed = summed - dot(chain[pair_index(current, earlier)], partial[earlier], 0, 0)
        partial.append(summed)
        if rows:
            summed, rows[-1] = lax.optimization_barrier((summed, rows[-1]))
        rows.append(lax.psum(summed, "row"))
        own_panel = lax.dynamic_slice_in_dim(panels[current], inner_part * col_cells, col_cells, 1)
        for earlier in range(current + 1):
            total[earlier, current] = dot(rows[earlier], own_panel, 1, 1)
    keys = sorted(total)
    stacked = jnp.stack([total[key] for key in keys])
    stacked = lax.psum(jnp.where(is_root, stacked, 0.0), ("row", "col"))
    total = {key: stacked[place] for place, key in enumerate(keys)}
    state = finish(total, chain, diag)
    state = lax.dynamic_slice_in_dim(state, row_place * nb_rows, nb_rows, 1)
    new_rows = jnp.stack(
        [lax.dynamic_slice_in_dim(row, row_place * nb_rows, nb_rows, 0) for row in rows]
    )
    return new_rows, state


def solution(mesh):
    in_specs = (
        P("row", "col"),
        P(None, "row", "col"),
        P(None, "row", "col"),
        P(None, "row", None),
        P(),
    )
    out_specs = (P(None, "row", "col"), P(None, "row", None))
    return jax.shard_map(
        per_device, mesh=mesh, in_specs=in_specs, out_specs=out_specs, check_vma=False
    )
```

time: 671 us -> 559 us (0.83)
  waiting for transfers between devices: 488 us -> 431 us
  matrix products: 102 us -> 69.4 us
  other arithmetic: 28.5 us -> 8.92 us
  local copies, waits for them, and re-layouts: 14.4 us -> 33.1 us
  blocking collectives: 14.5 us -> 0 us
  starting transfers between devices: 8.29 us -> 0.28 us
    reduce_scatter x3 -> x0, waiting for transfers between devices: 48.2 us -> none  [per_device(): rows_now = -lax.psum_scatter(summed, 'row', scatter_dimension=0, tiled=True)]
    psum x6 -> x4, waiting for transfers between devices: 340 us -> 303 us  [the longest x3 174 us: per_device(): rows.append(lax.psum(summed, 'row'))]
    all_gather x1 -> x4, waiting for transfers between devices: 94.2 us -> 127 us  [the longest x3 71 us: per_device(): lax.all_gather(local[current], 'col', axis=0, tiled=True)]
    dot_general x20, matrix products: 102 us -> 69.4 us  [dot(): lax.dot_general(left, right, (((left_dim,), (right_dim,)), ((), ())), pre...]
    all_gather x1 -> x0, blocking collectives: 14.5 us -> none  [per_device(): lax.all_gather(chain_panels, 'col', axis=2, tiled=True)]
    reshape x0 -> x2, local copies, waits for them, and re-layouts: none -> 9.56 us  [per_device(): small = small.reshape(row_count, col_count, 2, NSUPER, nb_rows, nb_cols)]
    all_to_all x2 -> x0, starting transfers between devices: 7.3 us -> none  [per_device(): lax.all_to_all(jnp.stack(crossing), 'row', split_axis=2, concat_axis=1, t...]
  transfers between devices with their start and end apart: 12 -> 8, of which waited for: 11 -> 8; matrix products, arithmetic and copies ran while one was open for 13% -> 12% of each run, Pallas kernels for 0% -> 0%
where the time goes in v1:
time: 559 us; the launch traced here: 558 us
  waiting for transfers between devices  431 us (77%)
  matrix products  69.4 us (12%)
  local copies, waits for them, and re-layouts  33.1 us (6%)
  between operations  14.7 us (3%)
  other arithmetic  8.92 us (2%)
    psum x3, waiting for transfers between devices, per_device(): rows.append(lax.psum(summed, 'row'))  174 us
    psum x1, waiting for transfers between devices, per_device(): stacked = lax.psum(jnp.where(is_root, stacked, 0.0), ('row', 'col'))  128 us
    all_gather x3, waiting for transfers between devices, per_device(): lax.all_gather(local[current], 'col', axis=0, tiled=True)  71 us
    dot_general x20, matrix products, dot(): lax.dot_general(left, right, (((left_dim,), (right_dim,)), ((), ())), pre...  69.4 us
    all_gather x1, waiting for transfers between devices, per_device(): small = lax.all_gather(small, ('row', 'col'), axis=0, tiled=False)  56.1 us
  transfers between devices with their start and end apart: 8, of which 8 were waited for; matrix products, arithmetic and copies ran while one was open for 12% of the time, Pallas kernels for 0%

profile of v1, /device:TPU:0, one launch (start us, length us, event | category | flops | bytes accessed | tf_op | source)
XLA Modules:
  0.0 557.8 jit_solution(12427171837398854230)
XLA Ops:
  13.4 56.1 %all-gather.8.cloned.1.call-done = f32[32,96,128]{2,1,0:T(8,128)} async-done(((f32[1,96,128]{2,1,0:T(8,128)}), f32[32,96,128]{2,1,0:T(8,128)}) %all-gather.8.cloned.1.call-update) | async-done | bytes 1572880 | tf_op jit(solution)/shard_map/all_gather | solution.py:74
  69.4 5.0 reshape.29
  74.5 4.5 copy.90
  83.4 24.9 %all-gather.14.cloned.1.call-done = f32[1,256,3072]{2,1,0:T(8,128)} async-done(((f32[1,32,3072]{2,1,0:T(8,128)}), f32[1,256,3072]{2,1,0:T(8,128)}) %all-gather.14.cloned.1.call-update) | async-done | bytes 3145744 | tf_op jit(solution)/shard_map/all_gather | solution.py:70
  108.3 14.5 %fusion.12 = f32[256,1536]{1,0:T(8,128)} fusion(f32[3072,1536]{1,0:T(8,128)} %param.5, f32[1,256,3072]{2,1,0:T(8,128)} %all-gather.14.cloned.1.call-done), kind=kOutput, calls=%fused_computation.11 | convolution fusion | flops 7248150528 | bytes 23592960 | tf_op jit(solution)/shard_map/dot_general | solution.py:16
  122.8 24.3 %all-gather.12.cloned.1.call-done = f32[1,256,3072]{2,1,0:T(8,128)} async-done(((f32[1,32,3072]{2,1,0:T(8,128)}), f32[1,256,3072]{2,1,0:T(8,128)}) %all-gather.12.cloned.1.call-update) | async-done | bytes 3145744 | tf_op jit(solution)/shard_map/all_gather | solution.py:70
  147.1 12.9 %fusion.9 = f32[256,1536]{1,0:T(8,128)S(1)} fusion(f32[3072,1536]{1,0:T(8,128)} %param.5, f32[1,256,3072]{2,1,0:T(8,128)} %all-gather.12.cloned.1.call-done), kind=kOutput, calls=%fused_computation.10 | convolution fusion | flops 7248150528 | bytes 23592960 | tf_op jit(solution)/shard_map/dot_general | solution.py:16
  160.0 4.0 convolution_subtract_fusion.1
  164.0 21.8 %all-gather.10.cloned.1.call-done = f32[1,256,3072]{2,1,0:T(8,128)} async-done(((f32[1,32,3072]{2,1,0:T(8,128)}), f32[1,256,3072]{2,1,0:T(8,128)}) %all-gather.10.cloned.1.call-update) | async-done | bytes 3145744 | tf_op jit(solution)/shard_map/all_gather | solution.py:70
  185.8 12.7 %fusion.6 = f32[256,1536]{1,0:T(8,128)S(1)} fusion(f32[3072,1536]{1,0:T(8,128)} %param.5, f32[1,256,3072]{2,1,0:T(8,128)} %all-gather.10.cloned.1.call-done), kind=kOutput, calls=%fused_computation.9 | convolution fusion | flops 7248150528 | bytes 23592960 | tf_op jit(solution)/shard_map/dot_general | solution.py:16
  201.5 3.5 convolution_subtract_fusion
  205.0 57.8 %all-reduce.5.cloned.1.call-done = f32[256,1536]{1,0:T(8,128)} async-done(((f32[256,1536]{1,0:T(8,128)}), f32[256,1536]{1,0:T(8,128)}) %all-reduce.5.cloned.1.call-update) | async-done | bytes 1572880 | tf_op jit(solution)/shard_map/psum | solution.py:90
  262.9 64.1 %all-reduce.7.cloned.1.call-done = f32[256,1536]{1,0:T(8,128)} async-done(((f32[256,1536]{1,0:T(8,128)}), f32[256,1536]{1,0:T(8,128)}) %all-reduce.7.cloned.1.call-update) | async-done | bytes 1572880 | tf_op jit(solution)/shard_map/psum | solution.py:90
  327.1 3.1 fusion.39
  330.3 3.1 fusion.45
  335.4 1.6 fusion.51
  338.6 52.4 %all-reduce.9.cloned.1.call-done = f32[256,1536]{1,0:T(8,128)} async-done(((f32[256,1536]{1,0:T(8,128)}), f32[256,1536]{1,0:T(8,128)}) %all-reduce.9.cloned.1.call-update) | async-done | bytes 1572880 | tf_op jit(solution)/shard_map/psum | solution.py:90
  391.0 2.9 fusion.69
  393.9 2.8 broadcast_select_fusion
  400.9 128.2 %all-reduce.11.cloned.1.call-done = f32[6,256,256]{2,1,0:T(8,128)} async-done(((f32[6,256,256]{2,1,0:T(8,128)}), f32[6,256,256]{2,1,0:T(8,128)}) %all-reduce.11.cloned.1.call-update) | async-done | bytes 1572880 | tf_op jit(solution)/shard_map/psum | solution.py:96
  529.2 2.0 fusion.85
  531.2 1.8 copy.119
  533.0 2.0 squeeze.66
  534.9 2.3 fusion.83
  (122 shorter events, 34.7 us)
Async XLA Ops:
  7.2 3.7 copy-start.23
  7.2 62.2 %all-gather.8.cloned.1.call-start = ((), (), s32[]{:S(2)}) async-start(), calls=%async_computation | async-start | bytes 1622016 | tf_op jit(solution)/shard_map/all_gather | solution.py:74
  10.0 98.3 %all-gather.14.cloned.1.call-start = ((), (), s32[]{:S(2)}) async-start(), calls=%async_computation.7 | async-start | bytes 3538944 | tf_op jit(solution)/shard_map/all_gather | solution.py:70
  12.1 135.0 %all-gather.12.cloned.1.call-start = ((), (), s32[]{:S(2)}) async-start(), calls=%async_computation.6 | async-start | bytes 3538944 | tf_op jit(solution)/shard_map/all_gather | solution.py:70
  12.8 173.0 %all-gather.10.cloned.1.call-start = ((), (), s32[]{:S(2)}) async-start(), calls=%async_computation.5 | async-start | bytes 3538944 | tf_op jit(solution)/shard_map/all_gather | solution.py:70
  79.0 2.0 copy-start.7
  81.7 78.4 %copy-start.11 = (f32[256,256]{0,1:T(8,128)}, f32[256,256]{0,1:T(8,128)S(1)}, u32[]{:S(2)}) copy-start(f32[256,256]{0,1:T(8,128)S(1)} %squeeze.61) | copy-start | bytes 786436
  160.0 38.5 %copy-start.2 = (f32[256,1536]{1,0:T(8,128)}, f32[256,1536]{1,0:T(8,128)S(1)}, u32[]{:S(2)}) copy-start(f32[256,1536]{1,0:T(8,128)S(1)} %fusion.9) | copy-start | bytes 4718596
  185.8 12.7 %copy-start.15 = (f32[256,256]{0,1:T(8,128)S(1)}, f32[256,256]{0,1:T(8,128)}, u32[]{:S(2)}) copy-start(f32[256,256]{0,1:T(8,128)} %squeeze.58) | copy-start | bytes 786436
  199.4 2.1 copy-start.6
  199.4 1.4 copy-start.18
  199.4 63.4 %all-reduce.5.cloned.1.call-start = ((), (), s32[]{:S(2)}) async-start(), calls=%async_computation.1 | async-start | bytes 3145728 | tf_op jit(solution)/shard_map/psum | solution.py:90
  201.5 3.5 copy-start.13
  205.0 122.0 %all-reduce.7.cloned.1.call-start = ((), (), s32[]{:S(2)}) async-start(), calls=%async_computation.2 | async-start | bytes 3145728 | tf_op jit(solution)/shard_map/psum | solution.py:90
  262.8 64.3 %copy-start.4 = (f32[256,1536]{1,0:T(8,128)S(1)}, f32[256,1536]{1,0:T(8,128)}, u32[]{:S(2)}) copy-start(f32[256,1536]{1,0:T(8,128)} %all-reduce.5.cloned.1.call-done) | copy-start | bytes 4718596
  262.9 128.2 %all-reduce.9.cloned.1.call-start = ((), (), s32[]{:S(2)}) async-start(), calls=%async_computation.3 | async-start | bytes 3145728 | tf_op jit(solution)/shard_map/psum | solution.py:90
  327.0 202.1 %all-reduce.11.cloned.1.call-start = ((), (), s32[]{:S(2)}) async-start(), calls=%async_computation.4 | async-start | bytes 3145728 | tf_op jit(solution)/shard_map/psum | solution.py:96
  327.1 3.1 copy-start.5
  327.1 7.8 %copy-start.10 = (f32[256,1536]{1,0:T(8,128)S(1)}, f32[256,1536]{1,0:T(8,128)}, u32[]{:S(2)}) copy-start(f32[256,1536]{1,0:T(8,128)} %all-reduce.7.cloned.1.call-done) | copy-start | bytes 4718596
  330.3 3.1 copy-start.3
  333.4 2.0 copy-start.9
  399.8 135.1 %copy-start.8 = (f32[4,8,2,3,64,32]{4,5,1,0,3,2:T(8,128)S(1)}, f32[4,8,2,3,64,32]{4,5,1,0,3,2:T(8,128)}, u32[]{:S(2)}) copy-start(f32[4,8,2,3,64,32]{4,5,1,0,3,2:T(8,128)} %copy-done.7) | copy-start | bytes 4718596
  544.6 3.6 copy-start.20
  546.0 2.9 copy-start.17
  (12 other events, 12.9 us)
Sparse Core Ops, SparseCore 0:
  11.6 57.7 all-gather.7
  71.1 37.1 all-gather.13
  109.9 37.1 all-gather.11
  148.6 37.1 all-gather.9
  203.0 59.7 all-reduce.4
  266.1 60.8 all-reduce.6
  330.1 60.8 all-reduce.8
  397.1 131.9 all-reduce.10

commit v2 on v1

v2 whole, which is shorter than its diff:
```python
import functools

import jax
import jax.numpy as jnp
from jax import lax
from jax.experimental import pallas as pl
from jax.experimental.pallas import tpu as pltpu
from jax.sharding import PartitionSpec as P

NB = 256
TILE = 128
NSUPER = 3
VMEM = pl.BlockSpec(memory_space=pltpu.VMEM)
VMEM_BYTES = 40 * 1024 * 1024


def pair_index(current, earlier):
    return current * (current - 1) // 2 + earlier


def total_index(earlier, current):
    return current * (current + 1) // 2 + earlier


def dot(left, right, left_dim, right_dim, precision=lax.Precision.HIGH):
    return lax.dot_general(
        left,
        right,
        (((left_dim,), (right_dim,)), ((), ())),
        precision=precision,
        preferred_element_type=jnp.float32,
    )


def send(source, target, sems, place, device):
    return pltpu.make_async_remote_copy(
        src_ref=source,
        dst_ref=target,
        send_sem=sems[0].at[place],
        recv_sem=sems[1].at[place],
        device_id=device,
        device_id_type=pl.DeviceIdType.MESH,
    )


def signal(device):
    pl.semaphore_signal(
        pltpu.get_barrier_semaphore(),
        inc=1,
        device_id=device,
        device_id_type=pl.DeviceIdType.MESH,
    )


def communicating(kernel, collective_id, out_shape, scratch_shapes, inputs):
    return pl.pallas_call(
        kernel,
        out_shape=out_shape,
        in_specs=[VMEM] * len(inputs),
        out_specs=jax.tree.map(lambda _: VMEM, out_shape),
        scratch_shapes=scratch_shapes,
        compiler_params=pltpu.CompilerParams(
            collective_id=collective_id, has_side_effects=True, vmem_limit_bytes=VMEM_BYTES
        ),
    )(*inputs)


def sem_pair(count):
    return [pltpu.SemaphoreType.DMA((count,)), pltpu.SemaphoreType.DMA((count,))]


def gather_kernel(
    row_count, col_count, chain, diag, all_chain, all_diag, s0, r0, s1, r1, s2, r2
):
    me_row, me_col = lax.axis_index("row"), lax.axis_index("col")
    for step in range(1, col_count):
        signal((me_row, lax.rem(me_col + step, col_count)))
    for step in range(1, row_count):
        signal((lax.rem(me_row + step, row_count), me_col))
    pl.semaphore_wait(pltpu.get_barrier_semaphore(), row_count + col_count - 2)
    copies = []
    for step in range(1, col_count):
        device = (me_row, lax.rem(me_col + step, col_count))
        copies.append(send(chain, all_chain.at[me_row, me_col], (s0, r0), step, device))
    later = []
    for step in range(1, row_count):
        device = (lax.rem(me_row + step, row_count), me_col)
        later.append(send(diag, all_diag.at[me_row], (s1, r1), step, device))
    for copy in copies + later:
        copy.start()
    all_chain[me_row, me_col] = chain[...]
    all_diag[me_row] = diag[...]
    for copy in copies:
        copy.wait()
    rows = []
    for step in range(1, row_count):
        device = (lax.rem(me_row + step, row_count), me_col)
        rows.append(send(all_chain.at[me_row], all_chain.at[me_row], (s2, r2), step, device))
    for copy in rows:
        copy.start()
    for copy in later + rows:
        copy.wait()


def row_sum_kernel(row_count, ratio, part, own, full, landed, s0, r0, s1, r1):
    me_row, me_col = lax.axis_index("row"), lax.axis_index("col")
    cells = own.shape[0]
    root = me_col // ratio

    def rows_of(place):
        return pl.ds(pl.multiple_of(place * cells, cells), cells)

    for step in range(1, row_count):
        signal((lax.rem(me_row + step, row_count), me_col))
    pl.semaphore_wait(pltpu.get_barrier_semaphore(), row_count - 1)
    copies = []
    for step in range(1, row_count):
        peer = lax.rem(me_row + step, row_count)
        copies.append(
            send(part.at[rows_of(peer)], landed.at[step], (s0, r0), step, (peer, me_col))
        )
    for copy in copies:
        copy.start()
    total = part[rows_of(me_row), :]
    for step, copy in enumerate(copies):
        copy.wait_recv()
        total = total + landed[step + 1]
    own[...] = total

    for step in range(1, row_count):
        peer = lax.rem(me_row + step, row_count)

        @pl.when(peer == root)
        def _():
            copy = send(own, full.at[rows_of(me_row)], (s1, r1), step, (peer, me_col))
            copy.start()
            copy.wait_send()

    @pl.when(me_row == root)
    def _():
        full[rows_of(me_row), :] = own[...]
        for step in range(1, row_count):
            peer = lax.rem(me_row + row_count - step, row_count)
            send(own, full.at[rows_of(peer)], (s1, r1), step, (peer, me_col)).wait_recv()

    for copy in copies:
        copy.wait_send()


def total_kernel(
    row_count, col_count, ratio, part, full, landed, s0, r0, s1, r1, s2, r2, s3, r3
):
    me_row, me_col = lax.axis_index("row"), lax.axis_index("col")
    cells = part.shape[0] // col_count
    half = col_count // 2
    root = me_col // ratio
    sibling = me_col + 1 - 2 * lax.rem(me_col, 2)

    def rows_of(place):
        return pl.ds(pl.multiple_of(place * cells, cells), cells)

    mine = full.at[rows_of(me_col)]
    for step in range(1, row_count):
        signal((lax.rem(me_row + step, row_count), me_col))
    for step in range(1, col_count):
        signal((me_row, lax.rem(me_col + step, col_count)))

    @pl.when(me_row != root)
    def _():
        pl.semaphore_wait(pltpu.get_barrier_semaphore(), row_count + col_count - 2)

    @pl.when(me_row == root)
    def _():
        for step in range(1, col_count):
            peer = lax.rem(me_col + step, col_count)
            signal((peer // ratio, peer))
        pl.semaphore_wait(pltpu.get_barrier_semaphore(), row_count + 2 * col_count - 3)
        copies = []
        for step in range(1, col_count):
            peer = lax.rem(me_col + step, col_count)
            copies.append(
                send(part.at[rows_of(peer)], landed.at[step], (s0, r0), step, (peer // ratio, peer))
            )
        for copy in copies:
            copy.start()
        total = part[rows_of(me_col), :]
        for step, copy in enumerate(copies):
            copy.wait_recv()
            total = total + landed[step + 1]
        full[rows_of(me_col), :] = total
        downs = []
        for step in range(1, row_count):
            device = (lax.rem(me_row + step, row_count), me_col)
            downs.append(send(mine, mine, (s1, r1), step, device))
        for copy in downs:
            copy.start()
        for copy in copies + downs:
            copy.wait_send()

    for step in range(1, row_count):
        peer = lax.rem(me_row + row_count - step, row_count)

        @pl.when(peer == root)
        def _():
            send(mine, mine, (s1, r1), step, (peer, me_col)).wait_recv()

    across = []
    for step in range(1, half):
        device = (me_row, lax.rem(me_col + 2 * step, col_count))
        across.append(send(mine, mine, (s2, r2), step, device))
    for copy in across:
        copy.start()
    beside = []
    for step in range(half):
        if step:
            across[step - 1].wait_recv()
        held = lax.rem(me_col + col_count - 2 * step, col_count)
        block = full.at[rows_of(held)]
        beside.append(send(block, block, (s3, r3), step, (me_row, sibling)))
        beside[-1].start()
    for copy in across:
        copy.wait_send()
    for copy in beside:
        copy.wait()


def finish_kernel(total, chain, diag, state):
    highest = lax.Precision.HIGHEST
    blocks = {}

    def total_of(earlier, current):
        return total[total_index(earlier, current) * NB : (total_index(earlier, current) + 1) * NB]

    for current in range(NSUPER):
        crossing = []
        for earlier in range(current):
            crossed = total_of(earlier, current)
            for middle in range(current):
                crossed = crossed + dot(
                    blocks[earlier, middle], chain[pair_index(current, middle)], 1, 0, highest
                )
            crossing.append(-crossed)
        own = diag[current] - total_of(current, current)
        for earlier in range(current):
            blocks[earlier, current] = crossing[earlier]
            blocks[current, earlier] = crossing[earlier].T
            own = own - dot(
                blocks[current, earlier], chain[pair_index(current, earlier)], 1, 0, highest
            )
        blocks[current, current] = own
    for line in range(NSUPER):
        for column in range(NSUPER):
            state[line, :, column * NB : (column + 1) * NB] = blocks[line, column]


def per_device(inverse_sep, sep_panels, chain_panels, diag_inverse, tile_list):
    row_count = lax.axis_size("row")
    col_count = lax.axis_size("col")
    row_place = lax.axis_index("row")
    col_place = lax.axis_index("col")
    row_cells, col_cells = inverse_sep.shape
    nb_rows = NB // row_count
    nb_cols = NB // col_count
    ratio_cols = col_count // row_count
    inner_part = col_place % ratio_cols
    tile_rows = row_cells // TILE
    listed = lax.dynamic_slice_in_dim(tile_list, row_place * tile_rows, tile_rows, 1)
    listed = jnp.repeat(listed.astype(jnp.float32), TILE, axis=1)

    local = jnp.swapaxes(sep_panels, 1, 2) * listed[:, None, :]
    panels = [
        lax.all_gather(local[current], "col", axis=0, tiled=True) for current in range(NSUPER)
    ]
    packed = chain_panels.reshape(-1, TILE)
    all_chain, all_diag = communicating(
        functools.partial(gather_kernel, row_count, col_count),
        0,
        (
            jax.ShapeDtypeStruct((row_count, col_count) + packed.shape, jnp.float32),
            jax.ShapeDtypeStruct((row_count,) + diag_inverse.shape, jnp.float32),
        ),
        sem_pair(col_count) + sem_pair(row_count) + sem_pair(row_count),
        (packed, diag_inverse),
    )
    chain = all_chain.reshape(row_count, col_count, NSUPER, nb_rows, nb_cols)
    chain = chain.transpose(2, 0, 3, 1, 4).reshape(NSUPER, NB, NB)
    diag = all_diag.transpose(1, 0, 2, 3).reshape(NSUPER, NB, NB)

    partial = []
    owns = []
    rows = []
    totals = []
    for current in range(NSUPER):
        summed = -dot(panels[current], inverse_sep, 1, 0)
        for earlier in range(current):
            summed = summed - dot(chain[pair_index(current, earlier)], partial[earlier], 0, 0)
        partial.append(summed)
        own, full = communicating(
            functools.partial(row_sum_kernel, row_count, ratio_cols),
            1 + current,
            (
                jax.ShapeDtypeStruct((nb_rows, col_cells), jnp.float32),
                jax.ShapeDtypeStruct((NB, col_cells), jnp.float32),
            ),
            [pltpu.VMEM((row_count, nb_rows, col_cells), jnp.float32)]
            + sem_pair(row_count)
            + sem_pair(row_count),
            (summed,),
        )
        owns.append(own)
        rows.append(full)
        own_panel = lax.dynamic_slice_in_dim(panels[current], inner_part * col_cells, col_cells, 1)
        for earlier in range(current + 1):
            totals.append(dot(rows[earlier], own_panel, 1, 1))
    part = jnp.concatenate(totals)
    total = communicating(
        functools.partial(total_kernel, row_count, col_count, ratio_cols),
        1 + NSUPER,
        jax.ShapeDtypeStruct(part.shape, jnp.float32),
        [pltpu.VMEM((col_count, part.shape[0] // col_count, NB), jnp.float32)]
        + sem_pair(col_count)
        + sem_pair(row_count)
        + sem_pair(col_count)
        + sem_pair(col_count),
        (part,),
    )
    state = pl.pallas_call(
        finish_kernel,
        out_shape=jax.ShapeDtypeStruct((NSUPER, NB, NSUPER * NB), jnp.float32),
        in_specs=[VMEM] * 3,
        out_specs=VMEM,
        compiler_params=pltpu.CompilerParams(vmem_limit_bytes=VMEM_BYTES),
    )(total, chain, diag)
    state = lax.dynamic_slice_in_dim(state, row_place * nb_rows, nb_rows, 1)
    return jnp.stack(owns), state


def solution(mesh):
    in_specs = (
        P("row", "col"),
        P(None, "row", "col"),
        P(None, "row", "col"),
        P(None, "row", None),
        P(),
    )
    out_specs = (P(None, "row", "col"), P(None, "row", None))
    return jax.shard_map(
        per_device, mesh=mesh, in_specs=in_specs, out_specs=out_specs, check_vma=False
    )
```

time: 559 us -> 289 us (0.52)
  waiting for transfers between devices: 431 us -> 1.4 us
  Pallas kernels: 0 us -> 194 us
  matrix products: 69.4 us -> 45.9 us
  other arithmetic: 8.92 us -> 3.22 us
  local copies, waits for them, and re-layouts: 33.1 us -> 27.5 us
    psum x4 -> x0, waiting for transfers between devices: 303 us -> none  [the longest x3 174 us: per_device(): rows.append(lax.psum(summed, 'row'))]
    pallas_call x0 -> x6, Pallas kernels: none -> 194 us  [the longest x5 191 us: communicating(): pl.pallas_call(kernel, out_shape=out_shape, in_specs=[VMEM] * len(inputs)...]
    all_gather x3, waiting for transfers between devices: 71 us -> 0.01 us  [per_device(): lax.all_gather(local[current], 'col', axis=0, tiled=True)]
    all_gather x1 -> x0, waiting for transfers between devices: 56.1 us -> none  [per_device(): small = lax.all_gather(small, ('row', 'col'), axis=0, tiled=False)]
    dot_general x20 -> x12, matrix products: 69.4 us -> 45.9 us  [dot(): lax.dot_general(left, right, (((left_dim,), (right_dim,)), ((), ())), pre...]
    slice x4, local copies, waits for them, and re-layouts: 2.38 us -> 8.43 us  [per_device(): chain[pair_index(current, earlier)]]
  transfers between devices with their start and end apart: 8 -> 3, of which waited for: 8 -> 0; matrix products, arithmetic and copies ran while one was open for 12% -> 16% of each run, Pallas kernels for 0% -> 35%
where the time goes in v2:
time: 289 us; the launch traced here: 286 us
  Pallas kernels  194 us (67%)
  matrix products  45.9 us (16%)
  local copies, waits for them, and re-layouts  27.5 us (10%)
  between operations  14.1 us (5%)
  other arithmetic  3.22 us (1%)
    pallas_call x5, Pallas kernels, communicating(): pl.pallas_call(kernel, out_shape=out_shape, in_specs=[VMEM] * len(inputs)...  191 us
    dot_general x12, matrix products, dot(): lax.dot_general(left, right, (((left_dim,), (right_dim,)), ((), ())), pre...  45.9 us
    slice x4, local copies, waits for them, and re-layouts, per_device(): chain[pair_index(current, earlier)]  8.43 us
    unnamed x35, local copies, waits for them, and re-layouts  6.06 us
  transfers between devices with their start and end apart: 3, of which 0 were waited for; matrix products, arithmetic and copies ran while one was open for 16% of the time, Pallas kernels for 35%

profile of v2, /device:TPU:0, one launch (start us, length us, event | category | flops | bytes accessed | tf_op | source)
XLA Modules:
  0.0 286.1 jit_solution(6667734811690196937)
XLA Ops:
  8.1 1.4 multiply_bitcast_fusion
  9.5 1.1 fusion.58
  12.3 24.8 %shard_map.69 = (f32[4,8,48,128]{3,2,1,0:T(8,128)S(1)}, f32[4,3,64,256]{3,2,1,0:T(8,128)S(1)}) custom-call(f32[48,128]{1,0:T(8,128)S(1)} %reshape.23.chain, f32[3,64,256]{2,1,0:T(8,128)S(1)} %copy-done.8), custom_call_target="tpu_custom_call" | custom-call | tf_op jit(solution)/shard_map/pallas_call | solution.py:56
  37.1 2.4 reshape.24
  39.5 2.4 copy.14
  41.9 3.7 %fusion.57 = (f32[1,4,64,8,32]{4,2,0,3,1:T(8,128)}, f32[1,4,64,8,32]{4,2,0,3,1:T(8,128)}, f32[1,4,64,8,32]{4,2,0,3,1:T(8,128)}) fusion(f32[3,4,64,8,32]{4,2,0,3,1:T(8,128)} %bitcast.86), kind=kLoop, calls=%fused_computation.48 | loop fusion | bytes 1572864 | tf_op jit(solution)/shard_map/slice | solution.py:296
  45.6 1.6 copy.11
  47.2 1.0 squeeze.20
  48.3 1.6 copy.12
  50.9 1.6 copy.13
  54.4 1.2 copy.16.chain
  55.5 1.0 copy.15
  56.6 12.8 %fusion.6.part = f32[256,1536]{1,0:T(8,128)S(1)} fusion(f32[3072,1536]{1,0:T(8,128)} %param.5, f32[1,256,3072]{2,1,0:T(8,128)} %all-gather.7.cloned.1.call-done), kind=kOutput, calls=%fused_computation.9 | convolution fusion | flops 7248150528 | bytes 23592960 | tf_op jit(solution)/shard_map/dot_general | solution.py:26
  69.4 37.8 %shard_map.68 = (f32[64,1536]{1,0:T(8,128)S(1)}, f32[256,1536]{1,0:T(8,128)S(1)}) custom-call(f32[256,1536]{1,0:T(8,128)S(1)} %fusion.6.part), custom_call_target="tpu_custom_call" | custom-call | tf_op jit(solution)/shard_map/pallas_call | solution.py:56
  107.2 1.1 copy-done
  108.4 12.8 %fusion.9 = f32[256,1536]{1,0:T(8,128)S(1)} fusion(f32[3072,1536]{1,0:T(8,128)} %param.5, f32[1,256,3072]{2,1,0:T(8,128)} %all-gather.9.cloned.1.call-done), kind=kOutput, calls=%fused_computation.10 | convolution fusion | flops 7248150528 | bytes 23592960 | tf_op jit(solution)/shard_map/dot_general | solution.py:26
  122.1 36.8 %shard_map.70 = (f32[64,1536]{1,0:T(8,128)S(1)}, f32[256,1536]{1,0:T(8,128)S(1)}) custom-call(f32[256,1536]{1,0:T(8,128)S(1)} %convolution_subtract_fusion.2.part), custom_call_target="tpu_custom_call" | custom-call | tf_op jit(solution)/shard_map/pallas_call | solution.py:56
  158.9 1.2 copy-done.2
  160.8 12.7 %fusion.12 = f32[256,1536]{1,0:T(8,128)S(1)} fusion(f32[3072,1536]{1,0:T(8,128)} %param.5, f32[1,256,3072]{2,1,0:T(8,128)} %all-gather.11.cloned.1.call-done), kind=kOutput, calls=%fused_computation.11 | convolution fusion | flops 7248150528 | bytes 23592960 | tf_op jit(solution)/shard_map/dot_general | solution.py:26
  175.4 38.0 %shard_map.71 = (f32[64,1536]{1,0:T(8,128)S(1)}, f32[256,1536]{1,0:T(8,128)S(1)}) custom-call(f32[256,1536]{1,0:T(8,128)S(1)} %convolution_subtract_fusion.part), custom_call_target="tpu_custom_call" | custom-call | tf_op jit(solution)/shard_map/pallas_call | solution.py:56
  217.5 1.0 copy-done.9
  221.1 53.8 %shard_map.72.total = f32[1536,256]{1,0:T(8,128)S(1)} custom-call(f32[1536,256]{1,0:T(8,128)S(1)} %fusion.48.part), custom_call_target="tpu_custom_call" | custom-call | tf_op jit(solution)/shard_map/pallas_call | solution.py:56
  275.0 2.5 shard_map.73
  278.4 1.1 pad_maximum_fusion
  (56 shorter events, 16.4 us)
Async XLA Ops:
  7.2 49.4 %all-gather.7.cloned.1.call-start = ((), (), s32[]{:S(2)}) async-start(), calls=%async_computation | async-start | bytes 3538944 | tf_op jit(solution)/shard_map/all_gather | solution.py:272
  9.4 2.6 copy-start.15
  9.5 2.8 copy-start.8
  10.6 97.8 %all-gather.9.cloned.1.call-start = ((), (), s32[]{:S(2)}) async-start(), calls=%async_computation.1 | async-start | bytes 3538944 | tf_op jit(solution)/shard_map/all_gather | solution.py:272
  11.3 149.5 %all-gather.11.cloned.1.call-start = ((), (), s32[]{:S(2)}) async-start(), calls=%async_computation.2 | async-start | bytes 3538944 | tf_op jit(solution)/shard_map/all_gather | solution.py:272
  107.2 1.2 copy-start
  108.4 12.8 %copy-start.14 = (f32[256,256]{0,1:T(8,128)S(1)}, f32[256,256]{0,1:T(8,128)}, u32[]{:S(2)}) copy-start(f32[256,256]{0,1:T(8,128)} %squeeze.20) | copy-start | bytes 786436
  158.9 1.2 copy-start.2
  160.1 0.8 copy-start.6
  160.8 12.7 %copy-start.12 = (f32[256,256]{0,1:T(8,128)S(1)}, f32[256,256]{0,1:T(8,128)}, u32[]{:S(2)}) copy-start(f32[256,256]{0,1:T(8,128)} %squeeze.22) | copy-start | bytes 786436
  173.6 1.0 copy-start.13
  174.5 38.9 %copy-start.11 = (f32[1,256,3072]{2,1,0:T(8,128)S(1)}, f32[1,256,3072]{2,1,0:T(8,128)}, u32[]{:S(2)}) copy-start(f32[1,256,3072]{2,1,0:T(8,128)} %all-gather.7.cloned.1.call-done) | copy-start | bytes 9437188
  175.3 38.0 %copy-start.1 = (f32[256,1536]{1,0:T(8,128)S(1)}, f32[256,1536]{1,0:T(8,128)}, u32[]{:S(2)}) copy-start(f32[256,1536]{1,0:T(8,128)} %copy-done) | copy-start | bytes 4718596
  213.4 1.9 copy-start.10
  215.3 1.4 copy-start.3
  216.7 1.9 copy-start.9
  221.1 53.9 %copy-start.4 = (f32[3,256,256]{2,1,0:T(8,128)S(1)}, f32[3,256,256]{2,1,0:T(8,128)}, u32[]{:S(2)}) copy-start(f32[3,256,256]{2,1,0:T(8,128)} %copy.16.chain) | copy-start | bytes 2359300
  221.1 53.9 %copy-start.5 = (f32[3,4,64,256]{3,2,1,0:T(8,128)S(1)}, f32[3,4,64,256]{3,2,1,0:T(8,128)}, u32[]{:S(2)}) copy-start(f32[3,4,64,256]{3,2,1,0:T(8,128)} %copy.15) | copy-start | bytes 2359300
  275.0 3.4 %copy-start.7 = (f32[64,1536]{1,0:T(8,128)S(1)}, f32[64,1536]{1,0:T(8,128)}, u32[]{:S(2)}) copy-start(f32[64,1536]{1,0:T(8,128)} %copy-done.6) | copy-start | bytes 1179652
Sparse Core Ops, SparseCore 0:
  10.7 40.9 all-gather.6
  53.9 37.1 all-gather.8
  92.7 37.1 all-gather.10
